TPU v7x, 768 devices: a whole 4x8x12 slice. The times are simulated.
768 devices in a mesh: tower: 24 (over z_lo, x, core), local: 32 (over y, z_hi).
Axes of the slice: x: 4, y: 8, z: 12 (z_hi: 4, z_lo: 3; z = z_hi * 3 + z_lo), core: 2. Of those that a mesh axis runs over, the one named last changes fastest.
Arguments:
- top_cot: bfloat16 [32, 384, 4096], P('local', 'tower'), may hold values from -6 to 6
- top_pre: bfloat16 [32, 384, 4096], P('local', 'tower'), may hold values from -6 to 6
- top_weight: bfloat16 [6144, 4096], P('tower'), may hold values from -0.078125 to 0.078125
- tower_pre: bfloat16 [32, 384, 6144], P('local', None, 'tower'), may hold values from -6 to 6
- tower_weight: bfloat16 [24, 1536, 256], P('tower'), may hold values from -0.15625 to 0.15625
- pooled: bfloat16 [32, 384, 24, 1536], P('local', None, 'tower'), may hold values from -6 to 6
- feature_ids: int32 [32, 384, 24, 12, 4], P('local', None, 'tower'), may hold values from 0 to 255
- bag_lengths: int32 [32, 384, 24, 12], P('local', None, 'tower'), may hold values from 1 to 4
- block_slot: int32 [96], replicated, may hold values from 0 to 95, each once
Outputs:
- top_grad: float32 [6144, 4096], P('tower', 'local')
- tower_grad: float32 [24, 1536, 256], P('tower', 'local')
- emb_grad: float32 [24, 96, 32, 128], P('tower', 'local')
Inputs may be any that keep to these rules, and one draw needn't show every extreme that they name: block_slot is a permutation of the 96 slots.
All inputs are finite; a program needn't handle non-finite values.
Results may differ from a plain program's by a relative error of at most 0.015.
Values may be sent and summed in bfloat16 or wider, within the bound.
A program may use at most 64 MiB of HBM per device.

v0:
```python
import math

import jax
import jax.numpy as jnp
from jax import lax
from jax.sharding import PartitionSpec as P

FROWS = 256


def gelu_value(values):
    return 0.5 * values * (1.0 + jax.scipy.special.erf(values / math.sqrt(2.0)))


def gelu_slope(values):
    return 0.5 * (1.0 + jax.scipy.special.erf(values / math.sqrt(2.0))) + values * jnp.exp(
        -0.5 * values * values
    ) / math.sqrt(2.0 * math.pi)


def make_delta(cot_rows, pre_rows):
    return (cot_rows.astype(jnp.float32) * gelu_slope(pre_rows.astype(jnp.float32))).astype(
        jnp.bfloat16
    )


def local(
    top_cot,
    top_pre,
    top_weight,
    tower_pre,
    tower_weight,
    pooled,
    feature_ids,
    bag_lengths,
    block_slot,
):
    group = tower_pre.shape[1]
    factor = 1.0 / math.sqrt(group * lax.axis_size("local"))
    pre_rows = tower_pre[0].astype(jnp.float32)
    compressed = gelu_value(pre_rows).astype(jnp.bfloat16)
    local_delta = make_delta(top_cot, top_pre)
    rows = lax.all_gather(local_delta, "tower", axis=1, tiled=True)[0]
    part = jnp.einsum("kd,fd->kf", rows, top_weight, preferred_element_type=jnp.float32)
    weights = jnp.einsum("kf,kd->fd", compressed, rows, preferred_element_type=jnp.float32)
    top_grad = lax.psum_scatter(weights * factor, "local", scatter_dimension=1, tiled=True)
    feature_grad = part.astype(jnp.bfloat16)
    tower_delta = (feature_grad.astype(jnp.float32) * gelu_slope(pre_rows)).astype(jnp.bfloat16)
    pool_rows = pooled[0, :, 0, :]
    tower_term = (
        jnp.einsum("gs,gw->sw", pool_rows, tower_delta, preferred_element_type=jnp.float32) * factor
    )
    tower_grad = lax.psum_scatter(tower_term, "local", scatter_dimension=0, tiled=True)
    pooled_grad = jnp.einsum(
        "gw,sw->gs", tower_delta, tower_weight[0], preferred_element_type=jnp.float32
    ).astype(jnp.bfloat16)
    feats = feature_ids.shape[3]
    bag = feature_ids.shape[4]
    embed = pooled_grad.shape[1] // feats
    pooled_grad = pooled_grad.reshape(group, feats, embed)
    ids_here = feature_ids[0, :, 0]
    lens_here = bag_lengths[0, :, 0]
    valid = jnp.arange(bag, dtype=jnp.int32)[None, None, :] < lens_here[:, :, None]
    table_rows = jnp.arange(FROWS, dtype=jnp.int32)
    hits = (ids_here[..., None] == table_rows[None, None, None, :]) & valid[..., None]
    counts = jnp.sum(hits.astype(jnp.float32), axis=2).astype(jnp.bfloat16)
    dense = jnp.einsum("gfr,gfe->fre", counts, pooled_grad, preferred_element_type=jnp.float32)
    nblk = block_slot.shape[0]
    blocks = dense.reshape(nblk, feats * FROWS // nblk, embed)
    inverse = jnp.argsort(block_slot)
    slotted = jnp.take(blocks, inverse, axis=0)
    emb_grad = lax.psum_scatter(slotted, "local", scatter_dimension=0, tiled=True)
    return (top_grad, tower_grad[None], emb_grad[None])


def solution(mesh):
    placed = (
        P("local", "tower", None),
        P("local", "tower", None),
        P("tower", None),
        P("local", None, "tower"),
        P("tower", None, None),
        P("local", None, "tower", None),
        P("local", None, "tower", None, None),
        P("local", None, "tower", None),
        P(),
    )
    return jax.shard_map(
        local,
        mesh=mesh,
        in_specs=placed,
        out_specs=(P("tower", "local"), P("tower", "local", None), P("tower", "local", None, None)),
        check_vma=False,
    )
```

profile of v0, /device:TPU:2, one launch (start us, length us, event | category | flops | bytes accessed | tf_op | source)
XLA Modules:
  0.0 875.5 jit_solution(4071096894513839312)
XLA Ops:
  7.2 0.0 all-gather.2.cloned.1.call-start
  7.2 1.9 fusion.40
  9.2 0.0 reduce-scatter.10.cloned.1.call-start
  9.2 110.5 %all-gather.2.cloned.1.call-done = bf16[1,384,4096]{2,1,0:T(8,128)(2,1)} async-done(((bf16[1,16,4096]{2,1,0:T(8,128)(2,1)}), bf16[1,384,4096]{2,1,0:T(8,128)(2,1)}) %all-gather.2.cloned.1.call-update) | async-done | bytes 3145744 | tf_op jit(solution)/shard_map/all_gather | solution.py:43
  119.7 2.9 fusion.17
  122.6 1.7 fusion.4
  124.4 3.1 copy.32
  127.6 0.0 reduce-scatter.10.cloned.1.call-update
  127.6 0.0 reduce-scatter.8.cloned.1.call-start
  127.7 2.5 sort.17
  130.3 8.9 %convert_reduce_fusion = bf16[384,12,256]{2,0,1:T(8,128)(2,1)} fusion(s32[384,12,4]{0,2,1:T(4,128)S(1)} %bitcast.68, pred[384,12,4]{0,2,1:T(4,128)(4,1)S(1)} %iota_compare_fusion.1), kind=kLoop, calls=%fused_computation.1 | loop fusion | flops 17694720 | bytes 2451456 | tf_op jit(solution)/shard_map/reduce_sum | solution.py:66
  139.1 1.5 convolution_convert_fusion
  140.7 1.7 copy.26
  142.4 3.7 fusion.49
  146.0 3.2 gather_fusion
  149.3 2.8 broadcast_select_fusion
  152.1 0.0 reduce-scatter.8.cloned.1.call-update
  152.1 0.0 reduce-scatter.6.cloned.1.call-start
  152.2 5.1 convolution_multiply_fusion
  157.4 223.0 %reduce-scatter.10.cloned.1.call-done = f32[48,256]{1,0:T(8,128)} async-done(((f32[1536,256]{1,0:T(8,128)}), f32[48,256]{1,0:T(8,128)}) %reduce-scatter.10.cloned.1.call-update) | async-done | bytes 49168
  380.3 0.9 copy.33
  381.2 0.7 copy.29
  381.9 240.5 %reduce-scatter.8.cloned.1.call-done = f32[3,32,128]{2,1,0:T(8,128)} async-done(((f32[96,32,128]{2,1,0:T(8,128)}), f32[3,32,128]{2,1,0:T(8,128)}) %reduce-scatter.8.cloned.1.call-update) | async-done | bytes 49168 | tf_op jit(solution)/shard_map/reduce_scatter | solution.py:72
  622.4 246.6 %reduce-scatter.6.cloned.1.call-done = f32[256,128]{1,0:T(8,128)} async-done(((f32[256,4096]{1,0:T(8,128)}), f32[256,128]{1,0:T(8,128)}) %reduce-scatter.6.cloned.1.call-update) | async-done | bytes 131088 | tf_op jit(solution)/shard_map/reduce_scatter | solution.py:46
  (22 shorter events, 0.1 us)
Async XLA Ops:
  7.2 112.5 %copy-start = (bf16[256,4096]{1,0:T(8,128)(2,1)S(1)}, bf16[256,4096]{1,0:T(8,128)(2,1)}, u32[]{:S(2)}) copy-start(bf16[256,4096]{1,0:T(8,128)(2,1)} %param.11) | copy-start | bytes 6291460
  7.2 112.5 %all-gather.2.cloned.1.call-start = ((), (), s32[]{:S(2)}) async-start(), calls=%async_computation.3 | async-start | bytes 3276800 | tf_op jit(solution)/shard_map/all_gather | solution.py:43
  9.1 113.5 %copy-start.1 = (bf16[1,384,1,1536]{3,1,2,0:T(8,128)(2,1)S(1)}, bf16[1,384,1,1536]{3,1,2,0:T(8,128)(2,1)}, u32[]{:S(2)}) copy-start(bf16[1,384,1,1536]{3,1,2,0:T(8,128)(2,1)} %param.14) | copy-start | bytes 3538948
  9.2 371.2 %reduce-scatter.10.cloned.1.call-start = ((), (), s32[]{:S(2)}) async-start(), calls=%async_computation.6 | async-start | bytes 1622016
  124.4 3.2 copy-start.5
  124.4 3.3 copy-start.6
  124.4 5.9 copy-start.4
  127.5 11.6 %copy-start.2 = (bf16[1,1536,256]{2,1,0:T(8,128)(2,1)S(1)}, bf16[1,1536,256]{2,1,0:T(8,128)(2,1)}, u32[]{:S(2)}) copy-start(bf16[1,1536,256]{2,1,0:T(8,128)(2,1)} %param.13) | copy-start | bytes 2359300
  127.6 494.8 %reduce-scatter.8.cloned.1.call-start = ((), (), s32[]{:S(2)}) async-start(), calls=%async_computation.5 | async-start | bytes 1622016 | tf_op jit(solution)/shard_map/reduce_scatter | solution.py:72
  149.3 2.9 copy-start.3
  152.1 716.8 %reduce-scatter.6.cloned.1.call-start = ((), (), s32[]{:S(2)}) async-start(), calls=%async_computation.4 | async-start | bytes 4325376 | tf_op jit(solution)/shard_map/reduce_scatter | solution.py:46
Sparse Core Ops, SparseCore 0:
  11.0 108.6 all-gather.1
  127.7 252.5 reduce-scatter.9
  386.7 235.5 reduce-scatter.7
  627.9 241.0 reduce-scatter.5
where the time goes:
time: 876 us; the launch traced here: 875 us
  waiting for transfers between devices  821 us (94%)
  other arithmetic  16.2 us (2%)
  matrix products  15 us (2%)
  between operations  13.9 us (2%)
  local copies, waits for them, and re-layouts  9.72 us (1%)
    reduce_scatter x1, waiting for transfers between devices, local(): lax.psum_scatter(weights * factor, 'local', scatter_dimension=1, tiled=True)  247 us
    reduce_scatter x1, waiting for transfers between devices, local(): lax.psum_scatter(slotted, 'local', scatter_dimension=0, tiled=True)  240 us
    unnamed x5, waiting for transfers between devices  223 us
    all_gather x1, waiting for transfers between devices, local(): rows = lax.all_gather(local_delta, 'tower', axis=1, tiled=True)[0]  111 us
  transfers between devices with their start and end apart: 4, of which 4 were waited for; matrix products, arithmetic and copies ran while one was open for 4% of the time, Pallas kernels for 0%

commit v1 on v0

v1 whole, which is shorter than its diff:
```python
import math

import jax
import jax.numpy as jnp
from jax import lax
from jax.experimental import pallas as pl
from jax.experimental.pallas import tpu as pltpu
from jax.sharding import PartitionSpec as P

MESH = pl.DeviceIdType.MESH
F32, BF16 = jnp.float32, jnp.bfloat16

NZL, NX, NC, NY, NZH = 3, 4, 2, 8, 4
TOPW, WOUT, FEATS, EMB, BAG, FROWS, BLK = 4096, 256, 12, 128, 4, 256, 32
GROUP, SLAB, NBLK = 384, 1536, 96
SHARD = GROUP // (NZL * NX * NC)
LANES = TOPW // (NY * NZH)
PHASES = NZH
OFF = (2, 1, 3, 0)
WIDE = NY * LANES
HALF_WIDE = WIDE // 2
TOW_ROWS = SLAB // (NY * NZH)
EMB_ROWS = NBLK * BLK // (NY * NZH)
FACTOR = 1.0 / math.sqrt(12288)


def gelu_value(values):
    return 0.5 * values * (1.0 + lax.erf(values / math.sqrt(2.0)))


def gelu_slope(values):
    return 0.5 * (1.0 + lax.erf(values / math.sqrt(2.0))) + values * jnp.exp(
        -0.5 * values * values
    ) / math.sqrt(2.0 * math.pi)


def wide_sum(*terms):
    total = terms[0].astype(F32)
    for term in terms[1:]:
        total = total + term.astype(F32)
    return total


def kernel(
    cot_hbm, pre_hbm, tower_pre_hbm, ids_hbm, lens_hbm, slot_hbm, weight_hbm, tower_weight_hbm,
    pooled_hbm, out_top, out_tow, out_emb,
    cot, pre, tower_pre, ids, lens, slot, rows, weight, tower_weight, pooled, pooled_t, comp_t, slope, part, delta_t, counts, dense, slotted,
    top, tow, emb, rb_top, rb_tow, rb_emb,
    zs_top, zb_top, zf_top, zy_tow, zs_tow, zb_tow, zf_tow, zy_emb, zs_emb, zb_emb, zf_emb,
    load_sem, weight_sem, zl_send, zl_recv, x_send, x_recv, n_send, n_recv, b_send, b_recv,
    y_send, y_recv, zh_send, zh_recv,
):
    t, l = lax.axis_index("tower"), lax.axis_index("local")
    core, x, zl = lax.rem(t, NC), lax.rem(lax.div(t, NC), NX), lax.div(t, NC * NX)
    y, zh = lax.div(l, NZH), lax.rem(l, NZH)

    def at_tower(zl_, x_, core_):
        return ((zl_ * NX + x_) * NC + core_, l)

    def at_local(y_, zh_):
        return (t, y_ * NZH + zh_)

    xp, xm = lax.rem(x + 1, NX), lax.rem(x + NX - 1, NX)
    xo = lax.rem(x + 2, NX)
    zl_next = [lax.rem(zl + d, NZL) for d in (1, 2)]
    zl_prev = [lax.rem(zl + NZL - d, NZL) for d in (1, 2)]
    y_next = [lax.rem(y + 1, NY), lax.rem(y + NY - 1, NY)]
    zh_next = [lax.rem(zh + 1, NZH), lax.rem(zh + NZH - 1, NZH)]
    dev_zl = [at_tower(zl_, x, core) for zl_ in zl_next]
    dev_x = [at_tower(zl, x_, core) for x_ in (xp, xm)]
    dev_sib = at_tower(zl, x, 1 - core)
    dev_y = [at_local(y_, zh) for y_ in y_next]
    dev_zh = [at_local(y, zh_) for zh_ in zh_next]

    barrier = pltpu.get_barrier_semaphore()
    peers = dev_zl + dev_x + [dev_sib] + dev_y + dev_zh
    for peer in peers:
        pl.semaphore_signal(barrier, inc=1, device_id=peer, device_id_type=MESH)

    def first_column(q, k):
        owner = lax.rem(y + k, NY) * NZH + lax.rem(zh + OFF[q], NZH)
        return pl.multiple_of(owner * LANES, LANES)

    def remote(src, dst, send, recv, device):
        return pltpu.make_async_remote_copy(
            src_ref=src, dst_ref=dst, send_sem=send, recv_sem=recv,
            device_id=device, device_id_type=MESH,
        )

    loads = [
        pltpu.make_async_copy(src, dst, load_sem.at[i])
        for i, (src, dst) in enumerate(
            [
                (cot_hbm, cot), (pre_hbm, pre), (tower_pre_hbm, tower_pre), (ids_hbm, ids),
                (lens_hbm, lens), (slot_hbm, slot), (pooled_hbm, pooled),
                (tower_weight_hbm, tower_weight),
            ]
        )
    ]
    load_cot, load_pre, load_tower_pre, load_ids, load_lens, load_slot, load_pool, load_tw = loads
    for load in loads[:6]:
        load.start()
    for q in range(PHASES):
        for k in range(NY):
            pltpu.make_async_copy(
                weight_hbm.at[:, pl.ds(first_column(q, k), LANES)],
                weight.at[q, :, pl.ds(k * LANES, LANES)],
                weight_sem.at[q],
            ).start()
    load_pool.start()
    load_tw.start()
    load_cot.wait()
    load_pre.wait()

    for q in range(PHASES):
        for k in range(NY):
            cols = pl.ds(first_column(q, k), LANES)
            value = cot[:, cols].astype(F32) * gelu_slope(pre[:, cols].astype(F32))
            rows[q, zl, x, core, :, pl.ds(k * LANES, LANES)] = value.astype(BF16)

    pl.semaphore_wait(barrier, len(peers))

    def zl_copy(q, d):
        here = rows.at[q, zl, x, core]
        return remote(here, here, zl_send.at[q, d], zl_recv.at[q, d], dev_zl[d])

    def zl_arrival(q, d):
        there = rows.at[q, zl_prev[d], x, core]
        return remote(there, there, zl_send.at[q, d], zl_recv.at[q, d], dev_zl[1 - d])

    def x_copy(q, d):
        here = rows.at[q, :, x, core]
        return remote(here, here, x_send.at[q, d], x_recv.at[q, d], dev_x[d])

    def x_arrival(q, d):
        there = rows.at[q, :, (xm, xp)[d], core]
        return remote(there, there, x_send.at[q, d], x_recv.at[q, d], dev_x[1 - d])

    def n_copy(q, d):
        there = rows.at[q, :, (xm, xp)[d], core, :, pl.ds(d * HALF_WIDE, HALF_WIDE)]
        return remote(there, there, n_send.at[q, d], n_recv.at[q, d], dev_x[d])

    def n_arrival(q, d):
        there = rows.at[q, :, xo, core, :, pl.ds(d * HALF_WIDE, HALF_WIDE)]
        return remote(there, there, n_send.at[q, d], n_recv.at[q, d], dev_x[1 - d])

    def b_copy(q):
        here = rows.at[q, :, :, core]
        return remote(here, here, b_send.at[q], b_recv.at[q], dev_sib)

    def b_arrival(q):
        there = rows.at[q, :, :, 1 - core]
        return remote(there, there, b_send.at[q], b_recv.at[q], dev_sib)

    def step_z(q):
        for d in range(2):
            zl_copy(q, d).start()

    def step_x(q):
        for d in range(2):
            zl_arrival(q, d).wait_recv()
        for d in range(2):
            x_copy(q, d).start()

    def step_n(q):
        for d in range(2):
            x_arrival(q, d).wait_recv()
            n_copy(q, d).start()

    def step_b(q):
        for d in range(2):
            n_arrival(q, d).wait_recv()
        b_copy(q).start()

    half_rows = [WOUT // 2] * PHASES + [NZH * TOW_ROWS // 2, NZH * EMB_ROWS // 2]

    def chunk(p, k):
        if p < PHASES:
            return top.at[p, k]
        y_ = lax.rem(y + k, NY)
        if p == PHASES:
            return tow.at[pl.ds(pl.multiple_of(y_ * (NZH * TOW_ROWS), 16), NZH * TOW_ROWS)]
        return emb.at[pl.ds(pl.multiple_of(y_ * (NZH * EMB_ROWS), 16), NZH * EMB_ROWS)]

    def landing(p, d, h):
        ref = rb_top.at[p, d, h] if p < PHASES else (rb_tow, rb_emb)[p - PHASES].at[d, h]
        return ref.at[pl.ds(0, half_rows[p])] if h == 0 else ref

    def half(p, d):
        return pl.ds(d * half_rows[p], half_rows[p])

    def y_copy(p, d, h):
        if h == 0:
            src = chunk(p, NY // 2).at[half(p, d)]
        else:
            src = chunk(p, NY // 2 - h if d == 0 else NY // 2 + h)
        return remote(src, landing(p, d, h), y_send.at[p, d, h], y_recv.at[p, d, h], dev_y[d])

    def step_s(p):
        for d in range(2):
            y_copy(p, d, 0).start()

    def step_h(p, h):
        for d in range(2):
            y_copy(p, d, h - 1).wait_recv()
            own = chunk(p, NY // 2 - h if d == 0 else NY // 2 + h)
            if h == 1:
                own = own.at[half(p, d)]
            own[...] = wide_sum(own[...], landing(p, d, h - 1)[...]).astype(BF16)
            y_copy(p, d, h).start()

    def y_total(p):
        last = NY // 2 - 1
        for d in range(2):
            y_copy(p, d, last).wait_recv()
        return wide_sum(chunk(p, 0)[...], landing(p, 0, last)[...], landing(p, 1, last)[...])

    def zh_copy(i, src, dst, d):
        return remote(src, dst, zh_send.at[i], zh_recv.at[i], dev_zh[d])

    top_halves = [pl.ds(d * (WOUT // 2), WOUT // 2) for d in range(2)]
    zc_top = [zh_copy(d, zs_top.at[0, top_halves[d]], zb_top.at[d], d) for d in range(2)]
    zc_top += [zh_copy(2 + d, zs_top.at[1 + d], zf_top.at[d], d) for d in range(2)]
    zc_tow = [zh_copy(4, zs_tow.at[0], zb_tow, 0)]
    zc_tow += [zh_copy(5 + d, zs_tow.at[1 + d], zf_tow.at[d], d) for d in range(2)]
    zc_emb = [zh_copy(7, zs_emb.at[0], zb_emb, 1)]
    zc_emb += [zh_copy(8 + d, zs_emb.at[1 + d], zf_emb.at[d], d) for d in range(2)]

    def step_f_top(q):
        total = y_total(q)
        if q == 0:
            zs_top[0] = total.astype(BF16)
            for d in range(2):
                zc_top[d].start()
        elif q < 3:
            d = q - 1
            zc_top[d].wait_recv()
            zs_top[q] = total.astype(BF16)
            zs_top[q, top_halves[d]] = wide_sum(
                total[d * (WOUT // 2) : (d + 1) * (WOUT // 2)], zb_top[d]
            ).astype(BF16)
            zc_top[q + 1].start()
        else:
            out_top[...] = total

    def blocks(ref, size, offset):
        first = lax.rem(zh + offset, NZH) * size
        return ref[pl.ds(pl.multiple_of(first, 16), size), :]

    def step_f_pair(p, zy, zs, size, copies, via):
        zy[...] = y_total(p)
        zs[0] = blocks(zy, size, 2).astype(BF16)
        copies[0].start()
        zs[2 - via] = blocks(zy, size, (1, 3)[1 - via]).astype(BF16)
        copies[2 - via].start()

    def step_g_pair(zy, zs, zb, size, copies, via):
        copies[0].wait_recv()
        zs[1 + via] = wide_sum(blocks(zy, size, (1, 3)[via]), zb[...]).astype(BF16)
        copies[1 + via].start()

    def prepare_pre():
        load_tower_pre.wait()
        values = tower_pre[...].astype(F32)
        slope[...] = gelu_slope(values)
        comp_t[...] = gelu_value(values).T.astype(BF16)

    def prepare_counts(first, last):
        size = 64
        if first == 0:
            load_ids.wait()
            load_lens.wait()

        def feature(f, carry):
            length = lens[f]
            masked = [jnp.where(j < length, ids[f, j : j + 1, :], -1) for j in range(BAG)]
            for part_ in range(FROWS // size):
                table = lax.broadcasted_iota(jnp.int32, (size, GROUP), 0) + part_ * size
                hits = [jnp.where(m == table, 1.0, 0.0) for m in masked]
                count = (hits[0] + hits[1]) + (hits[2] + hits[3])
                counts[f, pl.ds(part_ * size, size), :] = count.astype(BF16)
            return carry

        lax.fori_loop(first, last, feature, 0)

    def prepare_pooled(first, last):
        if first == 0:
            load_pool.wait()
        for c in range(first, last):
            block = pooled[:, c * EMB : (c + 1) * EMB].astype(F32)
            pooled_t[c * EMB : (c + 1) * EMB, :] = block.T.astype(BF16)

    def compute_phase(q):
        b_arrival(q).wait_recv()
        pltpu.make_async_copy(weight.at[q], weight.at[q], weight_sem.at[q]).wait()
        for k in range(0, NY, 2):
            deltas = rows[q, :, :, :, :, k * LANES : (k + 2) * LANES].reshape(GROUP, 2 * LANES)
            term = jnp.dot(comp_t[...], deltas, preferred_element_type=F32) * FACTOR
            top[q, k] = term[:, :LANES].astype(BF16)
            top[q, k + 1] = term[:, LANES:].astype(BF16)
        step_s(q)
        deltas = rows[q].reshape(GROUP, WIDE)
        product = lax.dot_general(
            deltas, weight[q], (((1,), (1,)), ((), ())), preferred_element_type=F32
        )
        part[...] = product if q == 0 else part[...] + product

    def compute_tow():
        feature_grad = part[...].astype(BF16).astype(F32)
        delta_t[...] = (feature_grad * slope[...]).astype(BF16)
        for c in range(0, SLAB, 256):
            term = jnp.dot(pooled_t[c : c + 256, :], delta_t[...], preferred_element_type=F32)
            tow[c : c + 256, :] = (term * FACTOR).astype(BF16)

    def compute_emb():
        load_tw.wait()
        for f in range(FEATS):
            grad = lax.dot_general(
                delta_t[...], tower_weight[f * EMB : (f + 1) * EMB, :],
                (((1,), (1,)), ((), ())), preferred_element_type=F32,
            ).astype(BF16)
            dense[f * FROWS : (f + 1) * FROWS, :] = jnp.dot(
                counts[f], grad, preferred_element_type=F32
            )
        load_slot.wait()
        numbers = lax.broadcasted_iota(jnp.int32, (NBLK, NBLK), 0)
        moves = jnp.where(slot[...] == numbers, 1.0, 0.0).astype(BF16)
        for i in range(0, BLK, 2):
            taken = [dense[pl.ds(i + j, NBLK, stride=BLK), :].astype(BF16) for j in range(2)]
            moved = jnp.dot(moves, jnp.concatenate(taken, 1), preferred_element_type=F32)
            for j in range(2):
                slotted[pl.ds(i + j, NBLK, stride=BLK), :] = moved[:, j * EMB : (j + 1) * EMB]
        emb[...] = slotted[...].astype(BF16)

    for q in range(PHASES):
        step_z(q)
    prepare_pre()
    step_x(0)
    prepare_counts(0, 4)
    step_x(1)
    step_n(0)
    prepare_counts(4, 8)
    step_x(2)
    step_b(0)
    step_n(1)
    prepare_counts(8, 12)
    step_x(3)
    step_b(1)
    step_n(2)
    compute_phase(0)
    prepare_pooled(0, 6)
    step_b(2)
    step_n(3)
    compute_phase(1)
    step_h(0, 1)
    prepare_pooled(6, 12)
    step_b(3)
    compute_phase(2)
    step_h(0, 2)
    step_h(1, 1)
    compute_phase(3)
    step_h(0, 3)
    step_h(1, 2)
    step_h(2, 1)
    compute_tow()
    step_s(4)
    step_f_top(0)
    step_h(1, 3)
    step_h(2, 2)
    step_h(3, 1)
    compute_emb()
    step_s(5)
    step_f_top(1)
    step_h(2, 3)
    step_h(3, 2)
    step_h(4, 1)
    step_f_top(2)
    step_h(3, 3)
    step_h(4, 2)
    step_h(5, 1)
    step_f_top(3)
    step_h(4, 3)
    step_h(5, 2)
    step_f_pair(4, zy_tow, zs_tow, TOW_ROWS, zc_tow, 0)
    step_h(5, 3)
    step_g_pair(zy_tow, zs_tow, zb_tow, TOW_ROWS, zc_tow, 0)
    for d in range(2):
        zc_top[2 + d].wait_recv()
    out_top[...] = wide_sum(out_top[...], zf_top[0], zf_top[1])
    step_f_pair(5, zy_emb, zs_emb, EMB_ROWS, zc_emb, 1)
    for d in range(2):
        zc_tow[1 + d].wait_recv()
    out_tow[...] = wide_sum(blocks(zy_tow, TOW_ROWS, 0), zf_tow[0], zf_tow[1])
    step_g_pair(zy_emb, zs_emb, zb_emb, EMB_ROWS, zc_emb, 1)
    for d in range(2):
        zc_emb[1 + d].wait_recv()
    out_emb[...] = wide_sum(blocks(zy_emb, EMB_ROWS, 0), zf_emb[0], zf_emb[1])

    for q in range(PHASES):
        for d in range(2):
            zl_copy(q, d).wait_send()
            x_copy(q, d).wait_send()
            n_copy(q, d).wait_send()
        b_copy(q).wait_send()
    for p in range(PHASES + 2):
        for d in range(2):
            for h in range(NY // 2):
                y_copy(p, d, h).wait_send()
    for copy in zc_top + zc_tow + zc_emb:
        copy.wait_send()


def local(
    top_cot, top_pre, top_weight, tower_pre, tower_weight, pooled, feature_ids, bag_lengths, block_slot
):
    ids = jnp.transpose(feature_ids[0, :, 0], (1, 2, 0))
    lens = jnp.transpose(bag_lengths[0], (2, 1, 0))
    vmem, hbm = pl.BlockSpec(memory_space=pltpu.VMEM), pl.BlockSpec(memory_space=pltpu.HBM)
    dma = pltpu.SemaphoreType.DMA
    pieces = PHASES + 2
    outs = pl.pallas_call(
        kernel,
        out_shape=(
            jax.ShapeDtypeStruct((WOUT, LANES), F32),
            jax.ShapeDtypeStruct((TOW_ROWS, WOUT), F32),
            jax.ShapeDtypeStruct((EMB_ROWS, EMB), F32),
        ),
        in_specs=[hbm] * 9,
        out_specs=(vmem, vmem, vmem),
        scratch_shapes=[
            pltpu.VMEM((SHARD, TOPW), BF16),
            pltpu.VMEM((SHARD, TOPW), BF16),
            pltpu.VMEM((GROUP, WOUT), BF16),
            pltpu.VMEM((FEATS, BAG, GROUP), jnp.int32),
            pltpu.VMEM((FEATS, 1, GROUP), jnp.int32),
            pltpu.VMEM((1, NBLK), jnp.int32),
            pltpu.VMEM((PHASES, NZL, NX, NC, SHARD, WIDE), BF16),
            pltpu.VMEM((PHASES, WOUT, WIDE), BF16),
            pltpu.VMEM((SLAB, WOUT), BF16),
            pltpu.VMEM((GROUP, SLAB), BF16),
            pltpu.VMEM((SLAB, GROUP), BF16),
            pltpu.VMEM((WOUT, GROUP), BF16),
            pltpu.VMEM((GROUP, WOUT), F32),
            pltpu.VMEM((GROUP, WOUT), F32),
            pltpu.VMEM((GROUP, WOUT), BF16),
            pltpu.VMEM((FEATS, FROWS, GROUP), BF16),
            pltpu.VMEM((FEATS * FROWS, EMB), F32),
            pltpu.VMEM((NBLK * BLK, EMB), F32),
            pltpu.VMEM((PHASES, NY, WOUT, LANES), BF16),
            pltpu.VMEM((SLAB, WOUT), BF16),
            pltpu.VMEM((NBLK * BLK, EMB), BF16),
            pltpu.VMEM((PHASES, 2, NY // 2, WOUT, LANES), BF16),
            pltpu.VMEM((2, NY // 2, NZH * TOW_ROWS, WOUT), BF16),
            pltpu.VMEM((2, NY // 2, NZH * EMB_ROWS, EMB), BF16),
            pltpu.VMEM((3, WOUT, LANES), BF16),
            pltpu.VMEM((2, WOUT // 2, LANES), BF16),
            pltpu.VMEM((2, WOUT, LANES), BF16),
            pltpu.VMEM((NZH * TOW_ROWS, WOUT), F32),
            pltpu.VMEM((3, TOW_ROWS, WOUT), BF16),
            pltpu.VMEM((TOW_ROWS, WOUT), BF16),
            pltpu.VMEM((2, TOW_ROWS, WOUT), BF16),
            pltpu.VMEM((NZH * EMB_ROWS, EMB), F32),
            pltpu.VMEM((3, EMB_ROWS, EMB), BF16),
            pltpu.VMEM((EMB_ROWS, EMB), BF16),
            pltpu.VMEM((2, EMB_ROWS, EMB), BF16),
            dma((8,)),
            dma((PHASES,)),
            dma((PHASES, 2)),
            dma((PHASES, 2)),
            dma((PHASES, 2)),
            dma((PHASES, 2)),
            dma((PHASES, 2)),
            dma((PHASES, 2)),
            dma((PHASES,)),
            dma((PHASES,)),
            dma((pieces, 2, NY // 2)),
            dma((pieces, 2, NY // 2)),
            dma((10,)),
            dma((10,)),
        ],
        compiler_params=pltpu.CompilerParams(
            collective_id=0, has_side_effects=True, vmem_limit_bytes=64 * 1024 * 1024
        ),
    )(
        top_cot[0], top_pre[0], tower_pre[0], ids, lens, block_slot.reshape(1, NBLK), top_weight,
        tower_weight[0], pooled[0, :, 0, :],
    )
    return outs[0], outs[1][None], outs[2].reshape(1, NBLK // (NY * NZH), BLK, EMB)


def solution(mesh):
    placed = (
        P("local", "tower", None),
        P("local", "tower", None),
        P("tower", None),
        P("local", None, "tower"),
        P("tower", None, None),
        P("local", None, "tower", None),
        P("local", None, "tower", None, None),
        P("local", None, "tower", None),
        P(),
    )
    return jax.shard_map(
        local,
        mesh=mesh,
        in_specs=placed,
        out_specs=(P("tower", "local"), P("tower", "local", None), P("tower", "local", None, None)),
        check_vma=False,
    )
```

time: 876 us -> 95.6 us (0.11)
  the two profiles are of different devices: /device:TPU:2 before, /device:TPU:8 now
where the time goes in v1:
time: 95.6 us; the launch traced here: 95.3 us
  Pallas kernels  90.3 us (94%)
  local copies, waits for them, and re-layouts  4.41 us (5%)
    pallas_call x1, Pallas kernels, local(): pl.pallas_call(kernel, out_shape=(jax.ShapeDtypeStruct((WOUT, LANES), F32...  90.3 us
    unnamed x3, local copies, waits for them, and re-layouts  4.41 us

profile of v1, /device:TPU:8, one launch (start us, length us, event | category | flops | bytes accessed | tf_op | source)
XLA Modules:
  0.0 95.3 jit_solution(1052504890798493892)
XLA Ops:
  0.6 90.3 %shard_map.112 = (f32[256,128]{1,0:T(8,128)}, f32[48,256]{1,0:T(8,128)}, f32[96,128]{1,0:T(8,128)}) custom-call(bf16[16,4096]{1,0:T(8,128)(2,1)} %bitcast.17, bf16[16,4096]{1,0:T(8,128)(2,1)} %bitcast.18, bf16[384,256]{1,0:T(8,128)(2,1)} %bitcast.16, s32[12,4,384]{2,1,0:T(4,128)} %bitcast.19, s32[12,1,384]{2,1,0:T(1,128)} %bitcast.22, s32[1,96]{1,0:T(1,128)} %bitcast.23, ...), custom_call_target="tpu_custom_call" | custom-call | tf_op jit(solution)/shard_map/pallas_call | solution.py:421
  90.9 1.6 %copy.15 = f32[256,128]{1,0:T(8,128)} copy(f32[256,128]{1,0:T(8,128)} %get-tuple-element.12) | data formatting | bytes 262144
  92.5 1.4 %copy.16 = f32[1,48,256]{2,1,0:T(8,128)} copy(f32[1,48,256]{2,1,0:T(8,128)} %bitcast.21) | data formatting | bytes 98304
  93.9 1.4 %copy.17 = f32[1,3,32,128]{3,2,1,0:T(8,128)} copy(f32[1,3,32,128]{3,2,1,0:T(8,128)} %bitcast.20) | data formatting | bytes 98304

commit v2 on v1

--- a/solution.py
+++ b/solution.py
@@ -15,10 +15,12 @@
 GROUP, SLAB, NBLK = 384, 1536, 96
 SHARD = GROUP // (NZL * NX * NC)
 LANES = TOPW // (NY * NZH)
-PHASES = NZH
+PARTS = NZH
 OFF = (2, 1, 3, 0)
-WIDE = NY * LANES
+WIDE = PARTS * LANES
 HALF_WIDE = WIDE // 2
+AWAY = (4, 3, 5, 2, 6, 1, 7, 0)
+GROUPS = ((0, 1), (1, 3), (3, 5), (5, 8))
 TOW_ROWS = SLAB // (NY * NZH)
 EMB_ROWS = NBLK * BLK // (NY * NZH)
 FACTOR = 1.0 / math.sqrt(12288)
@@ -74,8 +76,6 @@
 
     barrier = pltpu.get_barrier_semaphore()
     peers = dev_zl + dev_x + [dev_sib] + dev_y + dev_zh
-    for peer in peers:
-        pl.semaphore_signal(barrier, inc=1, device_id=peer, device_id_type=MESH)
 
     def first_column(q, k):
         owner = lax.rem(y + k, NY) * NZH + lax.rem(zh + OFF[q], NZH)
@@ -98,92 +98,101 @@
         )
     ]
     load_cot, load_pre, load_tower_pre, load_ids, load_lens, load_slot, load_pool, load_tw = loads
-    for load in loads[:6]:
-        load.start()
-    for q in range(PHASES):
-        for k in range(NY):
-            pltpu.make_async_copy(
-                weight_hbm.at[:, pl.ds(first_column(q, k), LANES)],
-                weight.at[q, :, pl.ds(k * LANES, LANES)],
-                weight_sem.at[q],
-            ).start()
-    load_pool.start()
-    load_tw.start()
-    load_cot.wait()
-    load_pre.wait()
-
-    for q in range(PHASES):
-        for k in range(NY):
-            cols = pl.ds(first_column(q, k), LANES)
-            value = cot[:, cols].astype(F32) * gelu_slope(pre[:, cols].astype(F32))
-            rows[q, zl, x, core, :, pl.ds(k * LANES, LANES)] = value.astype(BF16)
-
-    pl.semaphore_wait(barrier, len(peers))
-
-    def zl_copy(q, d):
-        here = rows.at[q, zl, x, core]
-        return remote(here, here, zl_send.at[q, d], zl_recv.at[q, d], dev_zl[d])
-
-    def zl_arrival(q, d):
-        there = rows.at[q, zl_prev[d], x, core]
-        return remote(there, there, zl_send.at[q, d], zl_recv.at[q, d], dev_zl[1 - d])
-
-    def x_copy(q, d):
-        here = rows.at[q, :, x, core]
-        return remote(here, here, x_send.at[q, d], x_recv.at[q, d], dev_x[d])
-
-    def x_arrival(q, d):
-        there = rows.at[q, :, (xm, xp)[d], core]
-        return remote(there, there, x_send.at[q, d], x_recv.at[q, d], dev_x[1 - d])
-
-    def n_copy(q, d):
-        there = rows.at[q, :, (xm, xp)[d], core, :, pl.ds(d * HALF_WIDE, HALF_WIDE)]
-        return remote(there, there, n_send.at[q, d], n_recv.at[q, d], dev_x[d])
-
-    def n_arrival(q, d):
-        there = rows.at[q, :, xo, core, :, pl.ds(d * HALF_WIDE, HALF_WIDE)]
-        return remote(there, there, n_send.at[q, d], n_recv.at[q, d], dev_x[1 - d])
-
-    def b_copy(q):
-        here = rows.at[q, :, :, core]
-        return remote(here, here, b_send.at[q], b_recv.at[q], dev_sib)
-
-    def b_arrival(q):
-        there = rows.at[q, :, :, 1 - core]
-        return remote(there, there, b_send.at[q], b_recv.at[q], dev_sib)
-
-    def step_z(q):
-        for d in range(2):
-            zl_copy(q, d).start()
-
-    def step_x(q):
-        for d in range(2):
-            zl_arrival(q, d).wait_recv()
-        for d in range(2):
-            x_copy(q, d).start()
-
-    def step_n(q):
-        for d in range(2):
-            x_arrival(q, d).wait_recv()
-            n_copy(q, d).start()
-
-    def step_b(q):
-        for d in range(2):
-            n_arrival(q, d).wait_recv()
-        b_copy(q).start()
-
-    half_rows = [WOUT // 2] * PHASES + [NZH * TOW_ROWS // 2, NZH * EMB_ROWS // 2]
+    load_cot.start()
+    load_pre.start()
+    for peer in peers:
+        pl.semaphore_signal(barrier, inc=1, device_id=peer, device_id_type=MESH)
+
+    def load_rest():
+        load_tower_pre.start()
+        load_ids.start()
+        load_lens.start()
+        for g, (first, last) in enumerate(GROUPS):
+            for j in range(first, last):
+                for q in range(PARTS):
+                    pltpu.make_async_copy(
+                        weight_hbm.at[:, pl.ds(first_column(q, AWAY[j]), LANES)],
+                        weight.at[j, :, pl.ds(q * LANES, LANES)],
+                        weight_sem.at[g],
+                    ).start()
+        load_pool.start()
+        load_tw.start()
+        load_slot.start()
+
+    def compute_delta(g):
+        for j in range(*GROUPS[g]):
+            for q in range(PARTS):
+                cols = pl.ds(first_column(q, AWAY[j]), LANES)
+                value = cot[:, cols].astype(F32) * gelu_slope(pre[:, cols].astype(F32))
+                rows[j, zl, x, core, :, pl.ds(q * LANES, LANES)] = value.astype(BF16)
+
+    def group(g):
+        first, last = GROUPS[g]
+        return rows.at[pl.ds(first, last - first)]
+
+    def zl_copy(g, d):
+        here = group(g).at[:, zl, x, core]
+        return remote(here, here, zl_send.at[g, d], zl_recv.at[g, d], dev_zl[d])
+
+    def zl_arrival(g, d):
+        there = group(g).at[:, zl_prev[d], x, core]
+        return remote(there, there, zl_send.at[g, d], zl_recv.at[g, d], dev_zl[1 - d])
+
+    def x_copy(g, d):
+        here = group(g).at[:, :, x, core]
+        return remote(here, here, x_send.at[g, d], x_recv.at[g, d], dev_x[d])
+
+    def x_arrival(g, d):
+        there = group(g).at[:, :, (xm, xp)[d], core]
+        return remote(there, there, x_send.at[g, d], x_recv.at[g, d], dev_x[1 - d])
+
+    def n_copy(g, d):
+        there = group(g).at[:, :, (xm, xp)[d], core, :, pl.ds(d * HALF_WIDE, HALF_WIDE)]
+        return remote(there, there, n_send.at[g, d], n_recv.at[g, d], dev_x[d])
+
+    def n_arrival(g, d):
+        there = group(g).at[:, :, xo, core, :, pl.ds(d * HALF_WIDE, HALF_WIDE)]
+        return remote(there, there, n_send.at[g, d], n_recv.at[g, d], dev_x[1 - d])
+
+    def b_copy(g):
+        here = group(g).at[:, :, :, core]
+        return remote(here, here, b_send.at[g], b_recv.at[g], dev_sib)
+
+    def b_arrival(g):
+        there = group(g).at[:, :, :, 1 - core]
+        return remote(there, there, b_send.at[g], b_recv.at[g], dev_sib)
+
+    def step_z(g):
+        for d in range(2):
+            zl_copy(g, d).start()
+
+    def step_x(g):
+        for d in range(2):
+            zl_arrival(g, d).wait_recv()
+        for d in range(2):
+            x_copy(g, d).start()
+
+    def step_n(g, d):
+        x_arrival(g, d).wait_recv()
+        n_copy(g, d).start()
+
+    def step_b(g):
+        for d in range(2):
+            n_arrival(g, d).wait_recv()
+        b_copy(g).start()
+
+    half_rows = [WOUT // 2] * PARTS + [NZH * TOW_ROWS // 2, NZH * EMB_ROWS // 2]
 
     def chunk(p, k):
-        if p < PHASES:
+        if p < PARTS:
             return top.at[p, k]
         y_ = lax.rem(y + k, NY)
-        if p == PHASES:
+        if p == PARTS:
             return tow.at[pl.ds(pl.multiple_of(y_ * (NZH * TOW_ROWS), 16), NZH * TOW_ROWS)]
         return emb.at[pl.ds(pl.multiple_of(y_ * (NZH * EMB_ROWS), 16), NZH * EMB_ROWS)]
 
     def landing(p, d, h):
-        ref = rb_top.at[p, d, h] if p < PHASES else (rb_tow, rb_emb)[p - PHASES].at[d, h]
+        ref = rb_top.at[p, d, h] if p < PARTS else (rb_tow, rb_emb)[p - PARTS].at[d, h]
         return ref.at[pl.ds(0, half_rows[p])] if h == 0 else ref
 
     def half(p, d):
@@ -200,14 +209,13 @@
         for d in range(2):
             y_copy(p, d, 0).start()
 
-    def step_h(p, h):
-        for d in range(2):
-            y_copy(p, d, h - 1).wait_recv()
-            own = chunk(p, NY // 2 - h if d == 0 else NY // 2 + h)
-            if h == 1:
-                own = own.at[half(p, d)]
-            own[...] = wide_sum(own[...], landing(p, d, h - 1)[...]).astype(BF16)
-            y_copy(p, d, h).start()
+    def step_h(p, h, d):
+        y_copy(p, d, h - 1).wait_recv()
+        own = chunk(p, NY // 2 - h if d == 0 else NY // 2 + h)
+        if h == 1:
+            own = own.at[half(p, d)]
+        own[...] = wide_sum(own[...], landing(p, d, h - 1)[...]).astype(BF16)
+        y_copy(p, d, h).start()
 
     def y_total(p):
         last = NY // 2 - 1
@@ -290,20 +298,24 @@
             block = pooled[:, c * EMB : (c + 1) * EMB].astype(F32)
             pooled_t[c * EMB : (c + 1) * EMB, :] = block.T.astype(BF16)
 
-    def compute_phase(q):
-        b_arrival(q).wait_recv()
-        pltpu.make_async_copy(weight.at[q], weight.at[q], weight_sem.at[q]).wait()
-        for k in range(0, NY, 2):
-            deltas = rows[q, :, :, :, :, k * LANES : (k + 2) * LANES].reshape(GROUP, 2 * LANES)
+    def compute_top(g):
+        b_arrival(g).wait_recv()
+        for j in range(*GROUPS[g]):
+            deltas = rows[j].reshape(GROUP, WIDE)
             term = jnp.dot(comp_t[...], deltas, preferred_element_type=F32) * FACTOR
-            top[q, k] = term[:, :LANES].astype(BF16)
-            top[q, k + 1] = term[:, LANES:].astype(BF16)
-        step_s(q)
-        deltas = rows[q].reshape(GROUP, WIDE)
-        product = lax.dot_general(
-            deltas, weight[q], (((1,), (1,)), ((), ())), preferred_element_type=F32
-        )
-        part[...] = product if q == 0 else part[...] + product
+            for q in range(PARTS):
+                top[q, AWAY[j]] = term[:, q * LANES : (q + 1) * LANES].astype(BF16)
+
+    def compute_part(g):
+        first, last = GROUPS[g]
+        loaded = weight.at[pl.ds(first, last - first)]
+        pltpu.make_async_copy(loaded, loaded, weight_sem.at[g]).wait()
+        for j in range(first, last):
+            product = lax.dot_general(
+                rows[j].reshape(GROUP, WIDE), weight[j],
+                (((1,), (1,)), ((), ())), preferred_element_type=F32,
+            )
+            part[...] = product if j == 0 else part[...] + product
 
     def compute_tow():
         feature_grad = part[...].astype(BF16).astype(F32)
@@ -332,82 +344,133 @@
                 slotted[pl.ds(i + j, NBLK, stride=BLK), :] = moved[:, j * EMB : (j + 1) * EMB]
         emb[...] = slotted[...].astype(BF16)
 
-    for q in range(PHASES):
-        step_z(q)
+    load_cot.wait()
+    load_pre.wait()
+    compute_delta(0)
+    pl.semaphore_wait(barrier, len(peers))
+    step_z(0)
+    compute_delta(1)
+    step_z(1)
+    compute_delta(2)
+    step_z(2)
+    compute_delta(3)
+    step_z(3)
+    load_rest()
     prepare_pre()
     step_x(0)
     prepare_counts(0, 4)
     step_x(1)
-    step_n(0)
+    step_n(0, 0)
+    step_n(0, 1)
     prepare_counts(4, 8)
     step_x(2)
     step_b(0)
-    step_n(1)
+    step_n(1, 0)
+    step_n(1, 1)
+    step_x(3)
     prepare_counts(8, 12)
-    step_x(3)
+    compute_top(0)
+    for p in range(PARTS):
+        step_s(p)
     step_b(1)
-    step_n(2)
-    compute_phase(0)
+    step_n(2, 0)
+    step_n(2, 1)
     prepare_pooled(0, 6)
+    compute_top(1)
+    step_h(0, 1, 0)
+    step_h(0, 1, 1)
+    step_h(1, 1, 0)
+    step_h(1, 1, 1)
+    step_h(2, 1, 0)
+    step_h(2, 1, 1)
+    step_h(3, 1, 0)
+    step_h(3, 1, 1)
     step_b(2)
-    step_n(3)
-    compute_phase(1)
-    step_h(0, 1)
+    step_n(3, 0)
+    step_n(3, 1)
+    compute_part(0)
+    compute_part(1)
+    compute_top(2)
     prepare_pooled(6, 12)
+    step_h(0, 2, 0)
+    step_h(0, 2, 1)
+    step_h(1, 2, 0)
+    step_h(1, 2, 1)
     step_b(3)
-    compute_phase(2)
-    step_h(0, 2)
-    step_h(1, 1)
-    compute_phase(3)
-    step_h(0, 3)
-    step_h(1, 2)
-    step_h(2, 1)
+    compute_part(2)
+    step_h(2, 2, 0)
+    step_h(2, 2, 1)
+    step_h(3, 2, 0)
+    step_h(3, 2, 1)
+    compute_top(3)
+    compute_part(3)
     compute_tow()
     step_s(4)
-    step_f_top(0)
-    step_h(1, 3)
-    step_h(2, 2)
-    step_h(3, 1)
+    step_h(0, 3, 0)
+    step_h(0, 3, 1)
+    step_h(1, 3, 0)
+    step_h(1, 3, 1)
     compute_emb()
     step_s(5)
+    step_h(4, 1, 0)
+    step_h(4, 1, 1)
+    step_h(2, 3, 0)
+    step_h(2, 3, 1)
+    step_f_top(0)
+    step_h(5, 1, 0)
+    step_h(5, 1, 1)
+    step_h(4, 2, 0)
+    step_h(4, 2, 1)
     step_f_top(1)
-    step_h(2, 3)
-    step_h(3, 2)
-    step_h(4, 1)
+    step_h(5, 2, 0)
+    step_h(5, 2, 1)
     step_f_top(2)
-    step_h(3, 3)
-    step_h(4, 2)
-    step_h(5, 1)
+    step_h(4, 3, 0)
+    step_h(4, 3, 1)
+    step_h(5, 3, 0)
+    step_h(5, 3, 1)
+    step_h(3, 3, 0)
+    step_h(3, 3, 1)
+    step_f_pair(4, zy_tow, zs_tow, TOW_ROWS, zc_tow, 0)
+    step_f_pair(5, zy_emb, zs_emb, EMB_ROWS, zc_emb, 1)
+    step_g_pair(zy_tow, zs_tow, zb_tow, TOW_ROWS, zc_tow, 0)
+    step_g_pair(zy_emb, zs_emb, zb_emb, EMB_ROWS, zc_emb, 1)
+    for d in range(2):
+        zc_tow[1 + d].wait_recv()
+    out_tow[...] = wide_sum(blocks(zy_tow, TOW_ROWS, 0), zf_tow[0], zf_tow[1])
     step_f_top(3)
-    step_h(4, 3)
-    step_h(5, 2)
-    step_f_pair(4, zy_tow, zs_tow, TOW_ROWS, zc_tow, 0)
-    step_h(5, 3)
-    step_g_pair(zy_tow, zs_tow, zb_tow, TOW_ROWS, zc_tow, 0)
     for d in range(2):
         zc_top[2 + d].wait_recv()
     out_top[...] = wide_sum(out_top[...], zf_top[0], zf_top[1])
-    step_f_pair(5, zy_emb, zs_emb, EMB_ROWS, zc_emb, 1)
-    for d in range(2):
-        zc_tow[1 + d].wait_recv()
-    out_tow[...] = wide_sum(blocks(zy_tow, TOW_ROWS, 0), zf_tow[0], zf_tow[1])
-    step_g_pair(zy_emb, zs_emb, zb_emb, EMB_ROWS, zc_emb, 1)
     for d in range(2):
         zc_emb[1 + d].wait_recv()
     out_emb[...] = wide_sum(blocks(zy_emb, EMB_ROWS, 0), zf_emb[0], zf_emb[1])
 
-    for q in range(PHASES):
-        for d in range(2):
-            zl_copy(q, d).wait_send()
-            x_copy(q, d).wait_send()
-            n_copy(q, d).wait_send()
-        b_copy(q).wait_send()
-    for p in range(PHASES + 2):
+    for g in range(len(GROUPS)):
+        for d in range(2):
+            zl_copy(g, d).wait_send()
+            x_copy(g, d).wait_send()
+            n_copy(g, d).wait_send()
+        b_copy(g).wait_send()
+    for p in range(PARTS + 2):
         for d in range(2):
             for h in range(NY // 2):
                 y_copy(p, d, h).wait_send()
     for copy in zc_top + zc_tow + zc_emb:
         copy.wait_send()
+
+
+def place(*refs):
+    sources, results, held, sems = refs[:3], refs[3:6], refs[6:9], refs[9]
+    first = [pltpu.make_async_copy(*two, sems.at[0, i]) for i, two in enumerate(zip(sources, held))]
+    second = [pltpu.make_async_copy(*two, sems.at[1, i]) for i, two in enumerate(zip(held, results))]
+    for copy in first:
+        copy.start()
+    for one, two in zip(first, second):
+        one.wait()
+        two.start()
+    for copy in second:
+        copy.wait()
 
 
 def local(
@@ -417,14 +480,15 @@
     lens = jnp.transpose(bag_lengths[0], (2, 1, 0))
     vmem, hbm = pl.BlockSpec(memory_space=pltpu.VMEM), pl.BlockSpec(memory_space=pltpu.HBM)
     dma = pltpu.SemaphoreType.DMA
-    pieces = PHASES + 2
+    pieces = PARTS + 2
+    shapes = (
+        jax.ShapeDtypeStruct((WOUT, LANES), F32),
+        jax.ShapeDtypeStruct((TOW_ROWS, WOUT), F32),
+        jax.ShapeDtypeStruct((EMB_ROWS, EMB), F32),
+    )
     outs = pl.pallas_call(
         kernel,
-        out_shape=(
-            jax.ShapeDtypeStruct((WOUT, LANES), F32),
-            jax.ShapeDtypeStruct((TOW_ROWS, WOUT), F32),
-            jax.ShapeDtypeStruct((EMB_ROWS, EMB), F32),
-        ),
+        out_shape=shapes,
         in_specs=[hbm] * 9,
         out_specs=(vmem, vmem, vmem),
         scratch_shapes=[
@@ -434,8 +498,8 @@
             pltpu.VMEM((FEATS, BAG, GROUP), jnp.int32),
             pltpu.VMEM((FEATS, 1, GROUP), jnp.int32),
             pltpu.VMEM((1, NBLK), jnp.int32),
-            pltpu.VMEM((PHASES, NZL, NX, NC, SHARD, WIDE), BF16),
-            pltpu.VMEM((PHASES, WOUT, WIDE), BF16),
+            pltpu.VMEM((NY, NZL, NX, NC, SHARD, WIDE), BF16),
+            pltpu.VMEM((NY, WOUT, WIDE), BF16),
             pltpu.VMEM((SLAB, WOUT), BF16),
             pltpu.VMEM((GROUP, SLAB), BF16),
             pltpu.VMEM((SLAB, GROUP), BF16),
@@ -446,10 +510,10 @@
             pltpu.VMEM((FEATS, FROWS, GROUP), BF16),
             pltpu.VMEM((FEATS * FROWS, EMB), F32),
             pltpu.VMEM((NBLK * BLK, EMB), F32),
-            pltpu.VMEM((PHASES, NY, WOUT, LANES), BF16),
+            pltpu.VMEM((PARTS, NY, WOUT, LANES), BF16),
             pltpu.VMEM((SLAB, WOUT), BF16),
             pltpu.VMEM((NBLK * BLK, EMB), BF16),
-            pltpu.VMEM((PHASES, 2, NY // 2, WOUT, LANES), BF16),
+            pltpu.VMEM((PARTS, 2, NY // 2, WOUT, LANES), BF16),
             pltpu.VMEM((2, NY // 2, NZH * TOW_ROWS, WOUT), BF16),
             pltpu.VMEM((2, NY // 2, NZH * EMB_ROWS, EMB), BF16),
             pltpu.VMEM((3, WOUT, LANES), BF16),
@@ -464,15 +528,15 @@
             pltpu.VMEM((EMB_ROWS, EMB), BF16),
             pltpu.VMEM((2, EMB_ROWS, EMB), BF16),
             dma((8,)),
-            dma((PHASES,)),
-            dma((PHASES, 2)),
-            dma((PHASES, 2)),
-            dma((PHASES, 2)),
-            dma((PHASES, 2)),
-            dma((PHASES, 2)),
-            dma((PHASES, 2)),
-            dma((PHASES,)),
-            dma((PHASES,)),
+            dma((len(GROUPS),)),
+            dma((len(GROUPS), 2)),
+            dma((len(GROUPS), 2)),
+            dma((len(GROUPS), 2)),
+            dma((len(GROUPS), 2)),
+            dma((len(GROUPS), 2)),
+            dma((len(GROUPS), 2)),
+            dma((len(GROUPS),)),
+            dma((len(GROUPS),)),
             dma((pieces, 2, NY // 2)),
             dma((pieces, 2, NY // 2)),
             dma((10,)),
@@ -485,6 +549,14 @@
         top_cot[0], top_pre[0], tower_pre[0], ids, lens, block_slot.reshape(1, NBLK), top_weight,
         tower_weight[0], pooled[0, :, 0, :],
     )
+    outs = pl.pallas_call(
+        place,
+        out_shape=shapes,
+        in_specs=[hbm] * 3,
+        out_specs=(hbm, hbm, hbm),
+        scratch_shapes=[pltpu.VMEM(s.shape, F32) for s in shapes] + [dma((2, 3))],
+        compiler_params=pltpu.CompilerParams(vmem_limit_bytes=64 * 1024 * 1024),
+    )(*outs)
     return outs[0], outs[1][None], outs[2].reshape(1, NBLK // (NY * NZH), BLK, EMB)
 
 

time: 95.6 us -> 80.2 us (0.84)
  the two profiles are of different devices: /device:TPU:8 before, /device:TPU:1 now
where the time goes in v2:
time: 80.2 us; the launch traced here: 80 us
  Pallas kernels  79.4 us (99%)
    pallas_call x1, Pallas kernels, local(): pl.pallas_call(kernel, out_shape=shapes, in_specs=[hbm] * 9, out_specs=(v...  77.8 us
    pallas_call x1, Pallas kernels, local(): pl.pallas_call(place, out_shape=shapes, in_specs=[hbm] * 3, out_specs=(hb...  1.64 us

profile of v2, /device:TPU:1, one launch (start us, length us, event | category | flops | bytes accessed | tf_op | source)
XLA Modules:
  0.0 80.0 jit_solution(17003132138805487658)
XLA Ops:
  0.6 77.8 %shard_map.112 = (f32[256,128]{1,0:T(8,128)}, f32[48,256]{1,0:T(8,128)}, f32[96,128]{1,0:T(8,128)}) custom-call(bf16[16,4096]{1,0:T(8,128)(2,1)} %bitcast.17, bf16[16,4096]{1,0:T(8,128)(2,1)} %bitcast.18, bf16[384,256]{1,0:T(8,128)(2,1)} %bitcast.16, s32[12,4,384]{2,1,0:T(4,128)} %bitcast.19, s32[12,1,384]{2,1,0:T(1,128)} %bitcast.20, s32[1,96]{1,0:T(1,128)} %bitcast.21, ...), custom_call_target="tpu_custom_call" | custom-call | tf_op jit(solution)/shard_map/pallas_call | solution.py:489
  78.4 1.6 %shard_map.113 = (f32[256,128]{1,0:T(8,128)}, f32[48,256]{1,0:T(8,128)}, f32[96,128]{1,0:T(8,128)}) custom-call(f32[256,128]{1,0:T(8,128)} %get-tuple-element.9.refs_0_, f32[48,256]{1,0:T(8,128)} %get-tuple-element.10.refs_1_, f32[96,128]{1,0:T(8,128)} %get-tuple-element.11.refs_2_), custom_call_target="tpu_custom_call" | custom-call | tf_op jit(solution)/shard_map/pallas_call | solution.py:552

commit v3 on v2

--- a/solution.py
+++ b/solution.py
@@ -18,9 +18,9 @@
 PARTS = NZH
 OFF = (2, 1, 3, 0)
 WIDE = PARTS * LANES
-HALF_WIDE = WIDE // 2
 AWAY = (4, 3, 5, 2, 6, 1, 7, 0)
-GROUPS = ((0, 1), (1, 3), (3, 5), (5, 8))
+SPANS = ((0, 1), (1, 3), (3, 5), (5, 8))
+GROUPS = ((0, 0, 4), (1, 0, 4), (2, 0, 4), (3, 0, 4))
 TOW_ROWS = SLAB // (NY * NZH)
 EMB_ROWS = NBLK * BLK // (NY * NZH)
 FACTOR = 1.0 / math.sqrt(12288)
@@ -45,11 +45,12 @@
 
 def kernel(
     cot_hbm, pre_hbm, tower_pre_hbm, ids_hbm, lens_hbm, slot_hbm, weight_hbm, tower_weight_hbm,
-    pooled_hbm, out_top, out_tow, out_emb,
+    pooled_hbm, top_hbm, tow_hbm, emb_hbm,
+    out_top, out_tow, out_emb,
     cot, pre, tower_pre, ids, lens, slot, rows, weight, tower_weight, pooled, pooled_t, comp_t, slope, part, delta_t, counts, dense, slotted,
     top, tow, emb, rb_top, rb_tow, rb_emb,
-    zs_top, zb_top, zf_top, zy_tow, zs_tow, zb_tow, zf_tow, zy_emb, zs_emb, zb_emb, zf_emb,
-    load_sem, weight_sem, zl_send, zl_recv, x_send, x_recv, n_send, n_recv, b_send, b_recv,
+    zs_top, zb_top, zf_top, zy_tow, zs_tow, zf_tow, zy_emb, zs_emb, zf_emb,
+    load_sem, weight_sem, zl_send, zl_recv, x_send, x_recv, b_send, b_recv,
     y_send, y_recv, zh_send, zh_recv,
 ):
     t, l = lax.axis_index("tower"), lax.axis_index("local")
@@ -69,10 +70,12 @@
     y_next = [lax.rem(y + 1, NY), lax.rem(y + NY - 1, NY)]
     zh_next = [lax.rem(zh + 1, NZH), lax.rem(zh + NZH - 1, NZH)]
     dev_zl = [at_tower(zl_, x, core) for zl_ in zl_next]
-    dev_x = [at_tower(zl, x_, core) for x_ in (xp, xm)]
+    x_next, x_prev = (xp, xm, xo), (xm, xp, xo)
+    dev_x = [at_tower(zl, x_, core) for x_ in x_next]
+    dev_x_prev = [at_tower(zl, x_, core) for x_ in x_prev]
     dev_sib = at_tower(zl, x, 1 - core)
     dev_y = [at_local(y_, zh) for y_ in y_next]
-    dev_zh = [at_local(y, zh_) for zh_ in zh_next]
+    dev_zh = [at_local(y, zh_) for zh_ in zh_next + [lax.rem(zh + 2, NZH)]]
 
     barrier = pltpu.get_barrier_semaphore()
     peers = dev_zl + dev_x + [dev_sib] + dev_y + dev_zh
@@ -97,6 +100,12 @@
             ]
         )
     ]
+    put_top, put_tow, put_emb = [
+        pltpu.make_async_copy(src, dst, load_sem.at[8 + i])
+        for i, (src, dst) in enumerate(
+            [(out_top, top_hbm), (out_tow, tow_hbm), (out_emb, emb_hbm)]
+        )
+    ]
     load_cot, load_pre, load_tower_pre, load_ids, load_lens, load_slot, load_pool, load_tw = loads
     load_cot.start()
     load_pre.start()
@@ -107,7 +116,7 @@
         load_tower_pre.start()
         load_ids.start()
         load_lens.start()
-        for g, (first, last) in enumerate(GROUPS):
+        for g, (first, last) in enumerate(SPANS):
             for j in range(first, last):
                 for q in range(PARTS):
                     pltpu.make_async_copy(
@@ -120,46 +129,44 @@
         load_slot.start()
 
     def compute_delta(g):
-        for j in range(*GROUPS[g]):
-            for q in range(PARTS):
+        span, low, high = GROUPS[g]
+        for j in range(*SPANS[span]):
+            for q in range(low, high):
                 cols = pl.ds(first_column(q, AWAY[j]), LANES)
                 value = cot[:, cols].astype(F32) * gelu_slope(pre[:, cols].astype(F32))
                 rows[j, zl, x, core, :, pl.ds(q * LANES, LANES)] = value.astype(BF16)
 
-    def group(g):
-        first, last = GROUPS[g]
-        return rows.at[pl.ds(first, last - first)]
+    every = slice(None)
+
+    def group(g, zl_, x_, core_, piece=0, pieces=1):
+        span, low, high = GROUPS[g]
+        first, last = SPANS[span]
+        wide = (high - low) * LANES // pieces
+        cols = pl.ds(low * LANES + piece * wide, wide)
+        return rows.at[pl.ds(first, last - first), zl_, x_, core_, :, cols]
 
     def zl_copy(g, d):
-        here = group(g).at[:, zl, x, core]
+        here = group(g, zl, x, core)
         return remote(here, here, zl_send.at[g, d], zl_recv.at[g, d], dev_zl[d])
 
     def zl_arrival(g, d):
-        there = group(g).at[:, zl_prev[d], x, core]
+        there = group(g, zl_prev[d], x, core)
         return remote(there, there, zl_send.at[g, d], zl_recv.at[g, d], dev_zl[1 - d])
 
     def x_copy(g, d):
-        here = group(g).at[:, :, x, core]
+        here = group(g, every, x, core)
         return remote(here, here, x_send.at[g, d], x_recv.at[g, d], dev_x[d])
 
     def x_arrival(g, d):
-        there = group(g).at[:, :, (xm, xp)[d], core]
-        return remote(there, there, x_send.at[g, d], x_recv.at[g, d], dev_x[1 - d])
-
-    def n_copy(g, d):
-        there = group(g).at[:, :, (xm, xp)[d], core, :, pl.ds(d * HALF_WIDE, HALF_WIDE)]
-        return remote(there, there, n_send.at[g, d], n_recv.at[g, d], dev_x[d])
-
-    def n_arrival(g, d):
-        there = group(g).at[:, :, xo, core, :, pl.ds(d * HALF_WIDE, HALF_WIDE)]
-        return remote(there, there, n_send.at[g, d], n_recv.at[g, d], dev_x[1 - d])
+        there = group(g, every, x_prev[d], core)
+        return remote(there, there, x_send.at[g, d], x_recv.at[g, d], dev_x_prev[d])
 
     def b_copy(g):
-        here = group(g).at[:, :, :, core]
+        here = group(g, every, every, core)
         return remote(here, here, b_send.at[g], b_recv.at[g], dev_sib)
 
     def b_arrival(g):
-        there = group(g).at[:, :, :, 1 - core]
+        there = group(g, every, every, 1 - core)
         return remote(there, there, b_send.at[g], b_recv.at[g], dev_sib)
 
     def step_z(g):
@@ -169,16 +176,12 @@
     def step_x(g):
         for d in range(2):
             zl_arrival(g, d).wait_recv()
-        for d in range(2):
+        for d in range(3):
             x_copy(g, d).start()
 
-    def step_n(g, d):
-        x_arrival(g, d).wait_recv()
-        n_copy(g, d).start()
-
     def step_b(g):
-        for d in range(2):
-            n_arrival(g, d).wait_recv()
+        for d in range(3):
+            x_arrival(g, d).wait_recv()
         b_copy(g).start()
 
     half_rows = [WOUT // 2] * PARTS + [NZH * TOW_ROWS // 2, NZH * EMB_ROWS // 2]
@@ -229,10 +232,8 @@
     top_halves = [pl.ds(d * (WOUT // 2), WOUT // 2) for d in range(2)]
     zc_top = [zh_copy(d, zs_top.at[0, top_halves[d]], zb_top.at[d], d) for d in range(2)]
     zc_top += [zh_copy(2 + d, zs_top.at[1 + d], zf_top.at[d], d) for d in range(2)]
-    zc_tow = [zh_copy(4, zs_tow.at[0], zb_tow, 0)]
-    zc_tow += [zh_copy(5 + d, zs_tow.at[1 + d], zf_tow.at[d], d) for d in range(2)]
-    zc_emb = [zh_copy(7, zs_emb.at[0], zb_emb, 1)]
-    zc_emb += [zh_copy(8 + d, zs_emb.at[1 + d], zf_emb.at[d], d) for d in range(2)]
+    zc_tow = [zh_copy(4 + d, zs_tow.at[d], zf_tow.at[d], d) for d in range(3)]
+    zc_emb = [zh_copy(7 + d, zs_emb.at[d], zf_emb.at[d], d) for d in range(3)]
 
     def step_f_top(q):
         total = y_total(q)
@@ -255,17 +256,16 @@
         first = lax.rem(zh + offset, NZH) * size
         return ref[pl.ds(pl.multiple_of(first, 16), size), :]
 
-    def step_f_pair(p, zy, zs, size, copies, via):
+    def step_f_pair(p, zy, zs, size, copies):
         zy[...] = y_total(p)
-        zs[0] = blocks(zy, size, 2).astype(BF16)
-        copies[0].start()
-        zs[2 - via] = blocks(zy, size, (1, 3)[1 - via]).astype(BF16)
-        copies[2 - via].start()
-
-    def step_g_pair(zy, zs, zb, size, copies, via):
-        copies[0].wait_recv()
-        zs[1 + via] = wide_sum(blocks(zy, size, (1, 3)[via]), zb[...]).astype(BF16)
-        copies[1 + via].start()
+        for d in (2, 0, 1):
+            zs[d] = blocks(zy, size, (1, 3, 2)[d]).astype(BF16)
+            copies[d].start()
+
+    def finish_pair(out, zy, zf, size, copies):
+        for d in range(3):
+            copies[d].wait_recv()
+        out[...] = wide_sum(blocks(zy, size, 0), zf[0], zf[1], zf[2])
 
     def prepare_pre():
         load_tower_pre.wait()
@@ -299,17 +299,18 @@
             pooled_t[c * EMB : (c + 1) * EMB, :] = block.T.astype(BF16)
 
     def compute_top(g):
-        b_arrival(g).wait_recv()
-        for j in range(*GROUPS[g]):
-            deltas = rows[j].reshape(GROUP, WIDE)
-            term = jnp.dot(comp_t[...], deltas, preferred_element_type=F32) * FACTOR
-            for q in range(PARTS):
-                top[q, AWAY[j]] = term[:, q * LANES : (q + 1) * LANES].astype(BF16)
-
-    def compute_part(g):
-        first, last = GROUPS[g]
+        span, low, high = GROUPS[g]
+        for j in range(*SPANS[span]):
+            deltas = rows[j, :, :, :, :, low * LANES : high * LANES].reshape(GROUP, (high - low) * LANES)
+            term = (jnp.dot(comp_t[...], deltas, preferred_element_type=F32) * FACTOR).astype(BF16)
+            for q in range(low, high):
+                value = term[:, (q - low) * LANES : (q - low + 1) * LANES]
+                top[q, AWAY[j]] = value
+
+    def compute_part(i):
+        first, last = SPANS[i]
         loaded = weight.at[pl.ds(first, last - first)]
-        pltpu.make_async_copy(loaded, loaded, weight_sem.at[g]).wait()
+        pltpu.make_async_copy(loaded, loaded, weight_sem.at[i]).wait()
         for j in range(first, last):
             product = lax.dot_general(
                 rows[j].reshape(GROUP, WIDE), weight[j],
@@ -320,9 +321,13 @@
     def compute_tow():
         feature_grad = part[...].astype(BF16).astype(F32)
         delta_t[...] = (feature_grad * slope[...]).astype(BF16)
-        for c in range(0, SLAB, 256):
-            term = jnp.dot(pooled_t[c : c + 256, :], delta_t[...], preferred_element_type=F32)
-            tow[c : c + 256, :] = (term * FACTOR).astype(BF16)
+        for k in AWAY:
+            first = lax.rem(y + k, NY) * (NZH * TOW_ROWS)
+            here = pl.ds(pl.multiple_of(first, 16), NZH * TOW_ROWS)
+            term = jnp.dot(pooled_t[here, :], delta_t[...], preferred_element_type=F32)
+            tow[here, :] = (term * FACTOR).astype(BF16)
+            if k == NY // 2:
+                step_s(PARTS)
 
     def compute_emb():
         load_tw.wait()
@@ -342,7 +347,12 @@
             moved = jnp.dot(moves, jnp.concatenate(taken, 1), preferred_element_type=F32)
             for j in range(2):
                 slotted[pl.ds(i + j, NBLK, stride=BLK), :] = moved[:, j * EMB : (j + 1) * EMB]
-        emb[...] = slotted[...].astype(BF16)
+        for k in AWAY:
+            first = lax.rem(y + k, NY) * (NZH * EMB_ROWS)
+            here = pl.ds(pl.multiple_of(first, 16), NZH * EMB_ROWS)
+            emb[here, :] = slotted[here, :].astype(BF16)
+            if k == NY // 2:
+                step_s(PARTS + 1)
 
     load_cot.wait()
     load_pre.wait()
@@ -358,24 +368,20 @@
     load_rest()
     prepare_pre()
     step_x(0)
+    step_x(1)
     prepare_counts(0, 4)
-    step_x(1)
-    step_n(0, 0)
-    step_n(0, 1)
-    prepare_counts(4, 8)
     step_x(2)
     step_b(0)
-    step_n(1, 0)
-    step_n(1, 1)
     step_x(3)
-    prepare_counts(8, 12)
+    prepare_counts(4, 8)
+    b_arrival(0).wait_recv()
     compute_top(0)
     for p in range(PARTS):
         step_s(p)
     step_b(1)
-    step_n(2, 0)
-    step_n(2, 1)
+    prepare_counts(8, 12)
     prepare_pooled(0, 6)
+    b_arrival(1).wait_recv()
     compute_top(1)
     step_h(0, 1, 0)
     step_h(0, 1, 1)
@@ -386,32 +392,30 @@
     step_h(3, 1, 0)
     step_h(3, 1, 1)
     step_b(2)
-    step_n(3, 0)
-    step_n(3, 1)
     compute_part(0)
     compute_part(1)
+    prepare_pooled(6, 12)
+    b_arrival(2).wait_recv()
     compute_top(2)
-    prepare_pooled(6, 12)
+    step_b(3)
     step_h(0, 2, 0)
     step_h(0, 2, 1)
     step_h(1, 2, 0)
     step_h(1, 2, 1)
-    step_b(3)
     compute_part(2)
     step_h(2, 2, 0)
     step_h(2, 2, 1)
     step_h(3, 2, 0)
     step_h(3, 2, 1)
-    compute_top(3)
+    b_arrival(3).wait_recv()
     compute_part(3)
     compute_tow()
-    step_s(4)
+    compute_top(3)
     step_h(0, 3, 0)
     step_h(0, 3, 1)
     step_h(1, 3, 0)
     step_h(1, 3, 1)
     compute_emb()
-    step_s(5)
     step_h(4, 1, 0)
     step_h(4, 1, 1)
     step_h(2, 3, 0)
@@ -431,26 +435,26 @@
     step_h(5, 3, 1)
     step_h(3, 3, 0)
     step_h(3, 3, 1)
-    step_f_pair(4, zy_tow, zs_tow, TOW_ROWS, zc_tow, 0)
-    step_f_pair(5, zy_emb, zs_emb, EMB_ROWS, zc_emb, 1)
-    step_g_pair(zy_tow, zs_tow, zb_tow, TOW_ROWS, zc_tow, 0)
-    step_g_pair(zy_emb, zs_emb, zb_emb, EMB_ROWS, zc_emb, 1)
-    for d in range(2):
-        zc_tow[1 + d].wait_recv()
-    out_tow[...] = wide_sum(blocks(zy_tow, TOW_ROWS, 0), zf_tow[0], zf_tow[1])
+    step_f_pair(PARTS, zy_tow, zs_tow, TOW_ROWS, zc_tow)
+    step_f_pair(PARTS + 1, zy_emb, zs_emb, EMB_ROWS, zc_emb)
     step_f_top(3)
     for d in range(2):
         zc_top[2 + d].wait_recv()
     out_top[...] = wide_sum(out_top[...], zf_top[0], zf_top[1])
-    for d in range(2):
-        zc_emb[1 + d].wait_recv()
-    out_emb[...] = wide_sum(blocks(zy_emb, EMB_ROWS, 0), zf_emb[0], zf_emb[1])
-
+    put_top.start()
+    finish_pair(out_tow, zy_tow, zf_tow, TOW_ROWS, zc_tow)
+    put_tow.start()
+    finish_pair(out_emb, zy_emb, zf_emb, EMB_ROWS, zc_emb)
+    put_emb.start()
+
+    put_top.wait()
+    put_tow.wait()
+    put_emb.wait()
     for g in range(len(GROUPS)):
         for d in range(2):
             zl_copy(g, d).wait_send()
+        for d in range(3):
             x_copy(g, d).wait_send()
-            n_copy(g, d).wait_send()
         b_copy(g).wait_send()
     for p in range(PARTS + 2):
         for d in range(2):
@@ -478,7 +482,7 @@
 ):
     ids = jnp.transpose(feature_ids[0, :, 0], (1, 2, 0))
     lens = jnp.transpose(bag_lengths[0], (2, 1, 0))
-    vmem, hbm = pl.BlockSpec(memory_space=pltpu.VMEM), pl.BlockSpec(memory_space=pltpu.HBM)
+    hbm = pl.BlockSpec(memory_space=pltpu.HBM)
     dma = pltpu.SemaphoreType.DMA
     pieces = PARTS + 2
     shapes = (
@@ -490,8 +494,9 @@
         kernel,
         out_shape=shapes,
         in_specs=[hbm] * 9,
-        out_specs=(vmem, vmem, vmem),
-        scratch_shapes=[
+        out_specs=(hbm, hbm, hbm),
+        scratch_shapes=[pltpu.VMEM(s.shape, F32) for s in shapes]
+        + [
             pltpu.VMEM((SHARD, TOPW), BF16),
             pltpu.VMEM((SHARD, TOPW), BF16),
             pltpu.VMEM((GROUP, WOUT), BF16),
@@ -521,20 +526,16 @@
             pltpu.VMEM((2, WOUT, LANES), BF16),
             pltpu.VMEM((NZH * TOW_ROWS, WOUT), F32),
             pltpu.VMEM((3, TOW_ROWS, WOUT), BF16),
-            pltpu.VMEM((TOW_ROWS, WOUT), BF16),
-            pltpu.VMEM((2, TOW_ROWS, WOUT), BF16),
+            pltpu.VMEM((3, TOW_ROWS, WOUT), BF16),
             pltpu.VMEM((NZH * EMB_ROWS, EMB), F32),
             pltpu.VMEM((3, EMB_ROWS, EMB), BF16),
-            pltpu.VMEM((EMB_ROWS, EMB), BF16),
-            pltpu.VMEM((2, EMB_ROWS, EMB), BF16),
-            dma((8,)),
-            dma((len(GROUPS),)),
+            pltpu.VMEM((3, EMB_ROWS, EMB), BF16),
+            dma((11,)),
+            dma((len(SPANS),)),
             dma((len(GROUPS), 2)),
             dma((len(GROUPS), 2)),
-            dma((len(GROUPS), 2)),
-            dma((len(GROUPS), 2)),
-            dma((len(GROUPS), 2)),
-            dma((len(GROUPS), 2)),
+            dma((len(GROUPS), 3)),
+            dma((len(GROUPS), 3)),
             dma((len(GROUPS),)),
             dma((len(GROUPS),)),
             dma((pieces, 2, NY // 2)),

time: 80.2 us -> 78.9 us (0.984)
  the two profiles are of different devices: /device:TPU:1 before, /device:TPU:16 now
where the time goes in v3:
time: 78.9 us; the launch traced here: 78.7 us
  Pallas kernels  78.1 us (99%)
    pallas_call x1, Pallas kernels, local(): pl.pallas_call(kernel, out_shape=shapes, in_specs=[hbm] * 9, out_specs=(h...  76.4 us
    pallas_call x1, Pallas kernels, local(): pl.pallas_call(place, out_shape=shapes, in_specs=[hbm] * 3, out_specs=(hb...  1.64 us

profile of v3, /device:TPU:16, one launch (start us, length us, event | category | flops | bytes accessed | tf_op | source)
XLA Modules:
  0.0 78.7 jit_solution(11152160906581791123)
XLA Ops:
  0.6 76.4 %shard_map.112 = (f32[256,128]{1,0:T(8,128)}, f32[48,256]{1,0:T(8,128)}, f32[96,128]{1,0:T(8,128)}) custom-call(bf16[16,4096]{1,0:T(8,128)(2,1)} %bitcast.17, bf16[16,4096]{1,0:T(8,128)(2,1)} %bitcast.18, bf16[384,256]{1,0:T(8,128)(2,1)} %bitcast.16, s32[12,4,384]{2,1,0:T(4,128)} %bitcast.19, s32[12,1,384]{2,1,0:T(1,128)} %bitcast.20, s32[1,96]{1,0:T(1,128)} %bitcast.21, ...), custom_call_target="tpu_custom_call" | custom-call | tf_op jit(solution)/shard_map/pallas_call | solution.py:493
  77.1 1.6 %shard_map.113 = (f32[256,128]{1,0:T(8,128)}, f32[48,256]{1,0:T(8,128)}, f32[96,128]{1,0:T(8,128)}) custom-call(f32[256,128]{1,0:T(8,128)} %get-tuple-element.9.refs_0_, f32[48,256]{1,0:T(8,128)} %get-tuple-element.10.refs_1_, f32[96,128]{1,0:T(8,128)} %get-tuple-element.11.refs_2_), custom_call_target="tpu_custom_call" | custom-call | tf_op jit(solution)/shard_map/pallas_call | solution.py:553

commit v4 on v3

--- a/solution.py
+++ b/solution.py
@@ -116,17 +116,18 @@
         load_tower_pre.start()
         load_ids.start()
         load_lens.start()
-        for g, (first, last) in enumerate(SPANS):
-            for j in range(first, last):
-                for q in range(PARTS):
-                    pltpu.make_async_copy(
-                        weight_hbm.at[:, pl.ds(first_column(q, AWAY[j]), LANES)],
-                        weight.at[j, :, pl.ds(q * LANES, LANES)],
-                        weight_sem.at[g],
-                    ).start()
         load_pool.start()
         load_tw.start()
         load_slot.start()
+
+    def load_weight(g):
+        for j in range(*SPANS[g]):
+            for q in range(PARTS):
+                pltpu.make_async_copy(
+                    weight_hbm.at[:, pl.ds(first_column(q, AWAY[j]), LANES)],
+                    weight.at[j, :, pl.ds(q * LANES, LANES)],
+                    weight_sem.at[g],
+                ).start()
 
     def compute_delta(g):
         span, low, high = GROUPS[g]
@@ -153,13 +154,15 @@
         there = group(g, zl_prev[d], x, core)
         return remote(there, there, zl_send.at[g, d], zl_recv.at[g, d], dev_zl[1 - d])
 
-    def x_copy(g, d):
-        here = group(g, every, x, core)
-        return remote(here, here, x_send.at[g, d], x_recv.at[g, d], dev_x[d])
-
-    def x_arrival(g, d):
-        there = group(g, every, x_prev[d], core)
-        return remote(there, there, x_send.at[g, d], x_recv.at[g, d], dev_x_prev[d])
+    zl_held = [zl] + zl_prev
+
+    def x_copy(g, e, d):
+        here = group(g, zl_held[e], x, core)
+        return remote(here, here, x_send.at[g, e, d], x_recv.at[g, e, d], dev_x[d])
+
+    def x_arrival(g, e, d):
+        there = group(g, zl_held[e], x_prev[d], core)
+        return remote(there, there, x_send.at[g, e, d], x_recv.at[g, e, d], dev_x_prev[d])
 
     def b_copy(g):
         here = group(g, every, every, core)
@@ -172,16 +175,19 @@
     def step_z(g):
         for d in range(2):
             zl_copy(g, d).start()
+        for d in range(3):
+            x_copy(g, 0, d).start()
 
     def step_x(g):
-        for d in range(2):
-            zl_arrival(g, d).wait_recv()
-        for d in range(3):
-            x_copy(g, d).start()
+        for e in range(1, NZL):
+            zl_arrival(g, e - 1).wait_recv()
+            for d in range(3):
+                x_copy(g, e, d).start()
 
     def step_b(g):
-        for d in range(3):
-            x_arrival(g, d).wait_recv()
+        for e in range(NZL):
+            for d in range(3):
+                x_arrival(g, e, d).wait_recv()
         b_copy(g).start()
 
     half_rows = [WOUT // 2] * PARTS + [NZH * TOW_ROWS // 2, NZH * EMB_ROWS // 2]
@@ -367,20 +373,20 @@
     step_z(3)
     load_rest()
     prepare_pre()
+    prepare_counts(0, 4)
     step_x(0)
     step_x(1)
-    prepare_counts(0, 4)
     step_x(2)
     step_b(0)
     step_x(3)
-    prepare_counts(4, 8)
+    load_weight(0)
+    load_weight(1)
     b_arrival(0).wait_recv()
     compute_top(0)
     for p in range(PARTS):
         step_s(p)
     step_b(1)
-    prepare_counts(8, 12)
-    prepare_pooled(0, 6)
+    prepare_counts(4, 8)
     b_arrival(1).wait_recv()
     compute_top(1)
     step_h(0, 1, 0)
@@ -392,9 +398,11 @@
     step_h(3, 1, 0)
     step_h(3, 1, 1)
     step_b(2)
+    load_weight(2)
+    load_weight(3)
     compute_part(0)
     compute_part(1)
-    prepare_pooled(6, 12)
+    prepare_pooled(0, 6)
     b_arrival(2).wait_recv()
     compute_top(2)
     step_b(3)
@@ -403,10 +411,12 @@
     step_h(1, 2, 0)
     step_h(1, 2, 1)
     compute_part(2)
+    prepare_pooled(6, 12)
     step_h(2, 2, 0)
     step_h(2, 2, 1)
     step_h(3, 2, 0)
     step_h(3, 2, 1)
+    prepare_counts(8, 12)
     b_arrival(3).wait_recv()
     compute_part(3)
     compute_tow()
@@ -453,8 +463,9 @@
     for g in range(len(GROUPS)):
         for d in range(2):
             zl_copy(g, d).wait_send()
-        for d in range(3):
-            x_copy(g, d).wait_send()
+        for e in range(NZL):
+            for d in range(3):
+                x_copy(g, e, d).wait_send()
         b_copy(g).wait_send()
     for p in range(PARTS + 2):
         for d in range(2):
@@ -534,8 +545,8 @@
             dma((len(SPANS),)),
             dma((len(GROUPS), 2)),
             dma((len(GROUPS), 2)),
-            dma((len(GROUPS), 3)),
-            dma((len(GROUPS), 3)),
+            dma((len(GROUPS), NZL, 3)),
+            dma((len(GROUPS), NZL, 3)),
             dma((len(GROUPS),)),
             dma((len(GROUPS),)),
             dma((pieces, 2, NY // 2)),

time: 78.9 us -> 78.1 us (0.990)
  the two profiles are of different devices: /device:TPU:16 before, /device:TPU:8 now
where the time goes in v4:
time: 78.1 us; the launch traced here: 77.9 us
  Pallas kernels  77.3 us (99%)
    pallas_call x1, Pallas kernels, local(): pl.pallas_call(kernel, out_shape=shapes, in_specs=[hbm] * 9, out_specs=(h...  75.6 us
    pallas_call x1, Pallas kernels, local(): pl.pallas_call(place, out_shape=shapes, in_specs=[hbm] * 3, out_specs=(hb...  1.64 us

profile of v4, /device:TPU:8, one launch (start us, length us, event | category | flops | bytes accessed | tf_op | source)
XLA Modules:
  0.0 77.9 jit_solution(9266723310174054831)
XLA Ops:
  0.6 75.6 %shard_map.112 = (f32[256,128]{1,0:T(8,128)}, f32[48,256]{1,0:T(8,128)}, f32[96,128]{1,0:T(8,128)}) custom-call(bf16[16,4096]{1,0:T(8,128)(2,1)} %bitcast.17, bf16[16,4096]{1,0:T(8,128)(2,1)} %bitcast.18, bf16[384,256]{1,0:T(8,128)(2,1)} %bitcast.16, s32[12,4,384]{2,1,0:T(4,128)} %bitcast.19, s32[12,1,384]{2,1,0:T(1,128)} %bitcast.20, s32[1,96]{1,0:T(1,128)} %bitcast.21, ...), custom_call_target="tpu_custom_call" | custom-call | tf_op jit(solution)/shard_map/pallas_call | solution.py:504
  76.3 1.6 %shard_map.113 = (f32[256,128]{1,0:T(8,128)}, f32[48,256]{1,0:T(8,128)}, f32[96,128]{1,0:T(8,128)}) custom-call(f32[256,128]{1,0:T(8,128)} %get-tuple-element.9.refs_0_, f32[48,256]{1,0:T(8,128)} %get-tuple-element.10.refs_1_, f32[96,128]{1,0:T(8,128)} %get-tuple-element.11.refs_2_), custom_call_target="tpu_custom_call" | custom-call | tf_op jit(solution)/shard_map/pallas_call | solution.py:564
